TPU v7x, 128 devices: a whole 4x4x4 slice. The times are simulated.
128 devices in a mesh: tile: 16 (over y_hi, z, core), hid: 8 (over x, y_lo).
Axes of the slice: x: 4, y: 4 (y_hi: 2, y_lo: 2; y = y_hi * 2 + y_lo), z: 4, core: 2. Of those that a mesh axis runs over, the one named last changes fastest.
Arguments:
- residual_in: bfloat16 [8192, 6144], P('tile', 'hid'), may hold values from -68 to 68
- w_query: bfloat16 [6144, 3072], P('tile', 'hid'), may hold values from -0.078125 to 0.078125
- w_key: bfloat16 [6144, 3072], P('tile', 'hid'), may hold values from -0.078125 to 0.078125
- w_value: bfloat16 [6144, 3072], P('tile', 'hid'), may hold values from -0.078125 to 0.078125
- w_output: bfloat16 [3072, 6144], P('hid', 'tile'), may hold values from -0.109375 to 0.109375
- shift_mod: float32 [6144], replicated, may hold values from -4 to 4
- scale_mod: float32 [6144], replicated, may hold values from 0.5 to 11
- gate_mod: float32 [6144], replicated, may hold values from 0.5 to 1.5
- neighbours: int32 [256, 27], P('tile'), may hold values from -1 to 255, as said below
Outputs:
- block_out: bfloat16 [8192, 6144], P('tile', 'hid')
Inputs may be any that keep to these rules, and one draw needn't show every extreme that they name: `neighbours`: entry j of a tile's row is either -1 or the number of the tile at offset j; it is -1 where that tile lies outside the grid of 16 x 4 x 4 tiles (tile layers x tile rows x tile columns); the entry of offset 13 (the tile itself) is never -1.
All inputs are finite; a program needn't handle non-finite values.
Results may differ from a plain program's by a relative error of at most 0.02.
The roundings to bfloat16 on the way count: a program that leaves them out, or rounds other values in their place, can miss the bound.
Values may be sent and summed in bfloat16 or wider, within the bound.
No kernel may reach another device: no remote copies, remote signals or barrier semaphores. Data moves between devices by JAX's collectives and lax.ppermute only.
A program may use at most 128 MiB of HBM per device.

v0:
```python
import jax
import jax.numpy as jnp
import numpy as np
from jax import lax
from jax.sharding import PartitionSpec as P

HD = 128
TT = 2
TH = 4
TW = 4
HH = 16
WW = 16


def with_halo(shard, sides, width):
    for axis, dim in sides:
        size, length = (lax.axis_size(axis), shard.shape[dim])
        up = [(i, (i + 1) % size) for i in range(size - 1)]
        down = [(j, i) for i, j in up]
        last = lax.slice_in_dim(shard, length - width, length, axis=dim)
        first = lax.slice_in_dim(shard, 0, width, axis=dim)
        before = lax.ppermute(last, axis, up)
        after = lax.ppermute(first, axis, down)
        shard = jnp.concatenate([before, shard, after], axis=dim)
    return shard


def offset_table(per_row, per_col):
    per_layer = per_row * per_col
    table = np.zeros((per_layer, 3 * per_layer, 27), dtype=bool)
    for query_tile in range(per_layer):
        query_row, query_col = divmod(query_tile, per_col)
        for block_idx in range(3):
            for key_tile in range(per_layer):
                key_row, key_col = divmod(key_tile, per_col)
                row_step = key_row - query_row
                col_step = key_col - query_col
                if abs(row_step) <= 1 and abs(col_step) <= 1:
                    table[
                        query_tile,
                        block_idx * per_layer + key_tile,
                        block_idx * 9 + (row_step + 1) * 3 + (col_step + 1),
                    ] = True
    return table


def body(
    residual_in, w_query, w_key, w_value, w_output, shift_mod, scale_mod, gate_mod, neighbours
):
    tok_rows = residual_in.shape[0]
    feat_cols = residual_in.shape[1]
    hid_first = lax.axis_index("hid") * feat_cols
    whole = lax.all_gather(residual_in, "hid", axis=1, tiled=True)
    stream = whole.astype(jnp.float32)
    centre = jnp.mean(stream, axis=1, keepdims=True)
    spread = jnp.mean((stream - centre) * (stream - centre), axis=1, keepdims=True)
    normed = (stream - centre) * lax.rsqrt(spread + 1e-06)
    modded = (normed * (1.0 + scale_mod) + shift_mod).astype(jnp.bfloat16)
    head_cols = w_query.shape[1]
    query_sum = jnp.dot(
        modded,
        lax.all_gather(w_query, "tile", axis=0, tiled=True),
        preferred_element_type=jnp.float32,
    )
    key_sum = jnp.dot(
        modded,
        lax.all_gather(w_key, "tile", axis=0, tiled=True),
        preferred_element_type=jnp.float32,
    )
    value_sum = jnp.dot(
        modded,
        lax.all_gather(w_value, "tile", axis=0, tiled=True),
        preferred_element_type=jnp.float32,
    )
    queries = query_sum.astype(jnp.bfloat16)
    key_value = jnp.stack([key_sum.astype(jnp.bfloat16), value_sum.astype(jnp.bfloat16)])
    per_row = HH // TH
    per_col = WW // TW
    per_layer = per_row * per_col
    tile_len = TT * TH * TW
    layer_len = per_layer * tile_len
    layer_total = tok_rows // layer_len
    heads_dev = head_cols // HD
    bordered = with_halo(key_value, (("tile", 1),), layer_len)
    selector = jnp.asarray(offset_table(per_row, per_col))
    block_tiles = jnp.arange(3 * per_layer, dtype=jnp.int32)
    global_layer = lax.axis_index("tile") * layer_total + 0
    key_ids = (global_layer - 1 + block_tiles // per_layer) * per_layer + block_tiles % per_layer
    matches = (
        (neighbours[:, None, :] == key_ids[None, :, None])
        & (neighbours[:, None, :] >= 0)
        & selector
    )
    tile_mask = jnp.any(matches, axis=2)
    query_blk = queries.reshape(layer_len, heads_dev, HD)
    key_blk = bordered[0, 0 : 3 * layer_len].reshape(3 * layer_len, heads_dev, HD)
    value_blk = bordered[1, 0 : 3 * layer_len].reshape(3 * layer_len, heads_dev, HD)
    scores = jnp.einsum(
        "qhd,khd->hqk", query_blk, key_blk, preferred_element_type=jnp.float32
    ) * HD ** (-0.5)
    scores = scores.reshape(heads_dev, per_layer, tile_len, 3 * per_layer, tile_len)
    scores = jnp.where(tile_mask[None, :, None, :, None], scores, -1e30)
    scores = scores.reshape(heads_dev, layer_len, 3 * layer_len)
    peak_val = jnp.max(scores, axis=2, keepdims=True)
    chance = jnp.exp(scores - peak_val)
    denom_sum = jnp.sum(chance, axis=2)
    soft = chance.astype(jnp.bfloat16)
    blended = jnp.einsum("hqk,khd->qhd", soft, value_blk, preferred_element_type=jnp.float32)
    blended = blended / jnp.transpose(denom_sum)[:, :, None]
    pieces_out = blended.astype(jnp.bfloat16).reshape(layer_len, head_cols)
    partial_out = jnp.dot(
        pieces_out,
        lax.all_gather(w_output, "tile", axis=1, tiled=True),
        preferred_element_type=jnp.float32,
    )
    out_term = lax.psum_scatter(
        partial_out.astype(jnp.bfloat16), "hid", scatter_dimension=1, tiled=True
    ).astype(jnp.float32)
    gate_part = lax.dynamic_slice_in_dim(gate_mod, hid_first, feat_cols)
    return (residual_in.astype(jnp.float32) + gate_part * out_term).astype(jnp.bfloat16)


def solution(mesh):
    placed = (
        P("tile", "hid"),
        P("tile", "hid"),
        P("tile", "hid"),
        P("tile", "hid"),
        P("hid", "tile"),
        P(),
        P(),
        P(),
        P("tile", None),
    )
    return jax.shard_map(
        body, mesh=mesh, in_specs=placed, out_specs=P("tile", "hid"), check_vma=False
    )
```

profile of v0, /device:TPU:1, one launch (start us, length us, event | category | flops | bytes accessed | tf_op | source)
XLA Modules:
  0.0 529.0 jit_solution(9543873678163010500)
XLA Ops:
  6.5 0.0 all-gather.6.cloned.1.call-start
  6.5 0.7 all-gather.6.cloned.1.call-update
  7.3 0.0 all-gather.8.cloned.1.call-start
  7.3 0.7 all-gather.8.cloned.1.call-update
  8.0 0.0 all-gather.10.cloned.1.call-start
  8.1 0.7 all-gather.10.cloned.1.call-update
  8.7 0.0 all-gather.12.cloned.1.call-start
  8.8 0.5 all-gather.12.cloned.1.call-update
  9.3 0.0 all-gather.14.cloned.1.call-start
  9.4 0.5 all-gather.14.cloned.1.call-update
  9.9 0.0 reduce-scatter.2.cloned.1.call-start
  10.0 0.8 copy.19
  10.7 0.7 broadcast_compare_fusion
  11.4 0.7 broadcast_add_fusion
  12.2 0.1 copy.20
  12.3 1.0 and_reduce_fusion
  13.3 2.6 broadcast_in_dim.16
  15.9 7.8 %broadcast_in_dim.17 = pred[512,1536]{1,0:T(8,128)(4,1)S(1)} reshape(pred[16,32,48,32]{3,2,1,0:T(8,128)(4,1)} %broadcast_in_dim.16) | data formatting | bytes 1572864 | tf_op jit(solution)/shard_map/jit(_where)/broadcast_in_dim | solution.py:102
  23.7 117.6 %all-gather.6.cloned.1.call-done = bf16[512,6144]{1,0:T(8,128)(2,1)} async-done(((bf16[512,768]{1,0:T(8,128)(2,1)}), bf16[512,6144]{1,0:T(8,128)(2,1)}) %all-gather.6.cloned.1.call-update) | async-done | bytes 6291472 | tf_op jit(solution)/shard_map/all_gather | solution.py:53
  141.3 0.0 copy-start
  141.3 0.0 copy-start.3
  141.3 3.8 convert_reduce_fusion
  145.1 0.7 copy-done
  145.9 1.8 fusion.2
  147.6 0.0 copy-done.3
  147.6 6.3 %fusion.5 = bf16[512,6144]{1,0:T(8,128)(2,1)} fusion(bf16[512,6144]{1,0:T(8,128)(2,1)S(1)} %copy-done, f32[6144]{0:T(1024)S(1)} %copy-done.3, f32[6144]{0:T(1024)S(1)} %broadcast_add_fusion, f32[512]{0:T(512)S(1)} %add_rsqrt_fusion, f32[512]{0:T(512)S(1)} %broadcast_multiply_fusion), kind=kLoop, calls=%fused_computation.7 | loop fusion | flops 18874368 | bytes 12636160 | tf_op jit(solution)/shard_map/convert_element_type | solution.py:58
  154.0 49.4 %all-gather.8.cloned.1.call-done = bf16[6144,384]{1,0:T(8,128)(2,1)} async-done(((bf16[384,384]{1,0:T(8,128)(2,1)}), bf16[6144,384]{1,0:T(8,128)(2,1)}) %all-gather.8.cloned.1.call-update) | async-done | bytes 4718608 | tf_op jit(solution)/shard_map/all_gather | solution.py:67
  203.4 7.6 %fusion.15 = bf16[1,512,384]{2,1,0:T(8,128)(2,1)S(1)} fusion(bf16[512,6144]{1,0:T(8,128)(2,1)} %fusion.5, bf16[6144,384]{1,0:T(8,128)(2,1)} %all-gather.8.cloned.1.call-done), kind=kOutput, calls=%fused_computation.22 | convolution fusion | flops 2416115712 | bytes 11403264 | tf_op jit(solution)/shard_map/dot_general | solution.py:65
  211.0 50.4 %all-gather.10.cloned.1.call-done = bf16[6144,384]{1,0:T(8,128)(2,1)} async-done(((bf16[384,384]{1,0:T(8,128)(2,1)}), bf16[6144,384]{1,0:T(8,128)(2,1)}) %all-gather.10.cloned.1.call-update) | async-done | bytes 4718608 | tf_op jit(solution)/shard_map/all_gather | solution.py:72
  261.3 7.6 %fusion.16 = bf16[1,512,384]{2,1,0:T(8,128)(2,1)S(1)} fusion(bf16[512,6144]{1,0:T(8,128)(2,1)} %fusion.5, bf16[6144,384]{1,0:T(8,128)(2,1)} %all-gather.10.cloned.1.call-done), kind=kOutput, calls=%fused_computation.23 | convolution fusion | flops 2416115712 | bytes 11403264 | tf_op jit(solution)/shard_map/dot_general | solution.py:70
  268.9 1.0 pad_maximum_fusion.1
  269.9 1.9 collective-permute-start
  271.8 2.6 collective-permute-start.1
  274.4 51.4 %all-gather.12.cloned.1.call-done = bf16[6144,384]{1,0:T(8,128)(2,1)} async-done(((bf16[384,384]{1,0:T(8,128)(2,1)}), bf16[6144,384]{1,0:T(8,128)(2,1)}) %all-gather.12.cloned.1.call-update) | async-done | bytes 4718608 | tf_op jit(solution)/shard_map/all_gather | solution.py:62
  325.9 6.8 %convolution_convert_fusion.1 = bf16[512,384]{0,1:T(8,128)(2,1)S(1)} fusion(bf16[512,6144]{1,0:T(8,128)(2,1)} %fusion.5, bf16[6144,384]{1,0:T(8,128)(2,1)} %all-gather.12.cloned.1.call-done), kind=kOutput, calls=%fused_computation.19 | convolution fusion | flops 2416115712 | bytes 11403264 | tf_op jit(solution)/shard_map/dot_general | solution.py:60
  332.7 0.0 collective-permute-done
  332.7 0.0 collective-permute-done.1
  332.7 0.2 pad_maximum_fusion
  332.9 1.3 fusion.28
  334.2 1.6 copy.21
  335.8 1.5 copy.18
  337.3 2.2 fusion.6
  339.5 0.0 copy-start.2
  339.5 2.9 fusion.7
  342.5 0.0 copy-done.2
  342.5 3.0 fusion.20
  345.5 39.6 %all-gather.14.cloned.1.call-done = bf16[384,6144]{1,0:T(8,128)(2,1)} async-done(((bf16[384,384]{1,0:T(8,128)(2,1)}), bf16[384,6144]{1,0:T(8,128)(2,1)}) %all-gather.14.cloned.1.call-update) | async-done | bytes 4718608 | tf_op jit(solution)/shard_map/all_gather | solution.py:113
  385.1 0.0 copy-start.1
  385.1 7.8 %convolution_convert_fusion = bf16[512,6144]{1,0:T(8,128)(2,1)} fusion(bf16[512,384]{0,1:T(8,128)(2,1)S(1)} %bitcast.31, bf16[384,6144]{1,0:T(8,128)(2,1)} %all-gather.14.cloned.1.call-done), kind=kOutput, calls=%fused_computation.10 | convolution fusion | flops 2419064832 | bytes 11403264 | tf_op jit(solution)/shard_map/dot_general | solution.py:111
  392.8 0.0 reduce-scatter.2.cloned.1.call-update
  392.9 0.8 dynamic_slice.3
  393.7 126.3 %reduce-scatter.2.cloned.1.call-done = bf16[512,768]{1,0:T(8,128)(2,1)} async-done(((bf16[512,6144]{1,0:T(8,128)(2,1)}), bf16[512,768]{1,0:T(8,128)(2,1)}) %reduce-scatter.2.cloned.1.call-update) | async-done | bytes 786448 | tf_op jit(solution)/shard_map/reduce_scatter | solution.py:116
  519.9 0.0 copy-done.1
  519.9 2.2 add_convert_fusion
  (3 shorter events, 0.0 us)
Async XLA Ops:
  6.5 134.7 %all-gather.6.cloned.1.call-start = ((), (), s32[]{:S(2)}) async-start(), calls=%async_computation.1 | async-start | bytes 7077888 | tf_op jit(solution)/shard_map/all_gather | solution.py:53
  7.3 196.2 %all-gather.8.cloned.1.call-start = ((), (), s32[]{:S(2)}) async-start(), calls=%async_computation.2 | async-start | bytes 5013504 | tf_op jit(solution)/shard_map/all_gather | solution.py:67
  8.0 253.3 %all-gather.10.cloned.1.call-start = ((), (), s32[]{:S(2)}) async-start(), calls=%async_computation.3 | async-start | bytes 5013504 | tf_op jit(solution)/shard_map/all_gather | solution.py:72
  8.7 317.1 %all-gather.12.cloned.1.call-start = ((), (), s32[]{:S(2)}) async-start(), calls=%async_computation.4 | async-start | bytes 5013504 | tf_op jit(solution)/shard_map/all_gather | solution.py:62
  9.3 375.8 %all-gather.14.cloned.1.call-start = ((), (), s32[]{:S(2)}) async-start(), calls=%async_computation.5 | async-start | bytes 5013504 | tf_op jit(solution)/shard_map/all_gather | solution.py:113
  9.9 510.0 %reduce-scatter.2.cloned.1.call-start = ((), (), s32[]{:S(2)}) async-start(), calls=%async_computation.6 | async-start | bytes 7077888 | tf_op jit(solution)/shard_map/reduce_scatter | solution.py:116
  141.3 4.6 copy-start
  141.3 6.4 %copy-start.3 = (f32[6144]{0:T(1024)S(1)}, f32[6144]{0:T(1024)}, u32[]{:S(2)}) copy-start(f32[6144]{0:T(1024)} %param.15) | copy-start | bytes 73732
  269.9 62.8 %collective-permute-start = (bf16[2,512,384]{2,1,0:T(8,128)(2,1)}, bf16[2,512,384]{2,1,0:T(8,128)(2,1)S(1)}, u32[]{:S(2)}, u32[]{:S(2)}) collective-permute-start(bf16[2,512,384]{2,1,0:T(8,128)(2,1)} %pad_maximum_fusion.1), channel_id=1, source_target_pairs={{0,8},{8,16},{16,24},{24,32},{32,40},{40,48},{48,56},{56,64},{64,7... | collective-permute-start | bytes 2359304 | tf_op jit(solution)/shard_map/ppermute | solution.py:22
  271.8 60.9 %collective-permute-start.1 = (bf16[2,512,384]{2,1,0:T(8,128)(2,1)}, bf16[2,512,384]{2,1,0:T(8,128)(2,1)S(1)}, u32[]{:S(2)}, u32[]{:S(2)}) collective-permute-start(bf16[2,512,384]{2,1,0:T(8,128)(2,1)} %pad_maximum_fusion.1), channel_id=1, source_target_pairs={{8,0},{16,8},{24,16},{32,24},{40,32},{48,40},{56,48},{64,56},{72,6... | collective-permute-start | bytes 2359304 | tf_op jit(solution)/shard_map/ppermute | solution.py:23
  339.5 2.9 copy-start.2
  385.1 134.8 %copy-start.1 = (bf16[512,768]{1,0:T(8,128)(2,1)S(1)}, bf16[512,768]{1,0:T(8,128)(2,1)}, u32[]{:S(2)}) copy-start(bf16[512,768]{1,0:T(8,128)(2,1)} %param.10) | copy-start | bytes 2359300
Sparse Core Ops, SparseCore 0:
  9.0 132.2 all-gather.5
  143.7 59.6 all-gather.7
  205.9 55.3 all-gather.9
  263.7 62.1 all-gather.11
  328.0 57.0 all-gather.13
  393.0 126.8 reduce-scatter.1
where the time goes:
time: 530 us; the launch traced here: 529 us
  waiting for transfers between devices  438 us (83%)
  matrix products  34.9 us (7%)
  other arithmetic  20.8 us (4%)
  local copies, waits for them, and re-layouts  17.2 us (3%)
  between operations  13.6 us (3%)
    reduce_scatter x1, waiting for transfers between devices, body(): lax.psum_scatter(partial_out.astype(jnp.bfloat16), 'hid', scatter_dimensi...  126 us
    all_gather x1, waiting for transfers between devices, body(): whole = lax.all_gather(residual_in, 'hid', axis=1, tiled=True)  118 us
    all_gather x1, waiting for transfers between devices, body(): lax.all_gather(w_query, 'tile', axis=0, tiled=True)  51.4 us
    all_gather x1, waiting for transfers between devices, body(): lax.all_gather(w_value, 'tile', axis=0, tiled=True)  50.4 us
    all_gather x1, waiting for transfers between devices, body(): lax.all_gather(w_key, 'tile', axis=0, tiled=True)  49.4 us
    all_gather x1, waiting for transfers between devices, body(): lax.all_gather(w_output, 'tile', axis=1, tiled=True)  39.6 us
  transfers between devices with their start and end apart: 8, of which 6 were waited for; matrix products, arithmetic and copies ran while one was open for 12% of the time, Pallas kernels for 0%

commit v1 on v0

v1 whole, which is shorter than its diff:
```python
import functools

import jax
import jax.numpy as jnp
import numpy as np
from jax import lax
from jax.experimental import pallas as pl
from jax.experimental.pallas import tpu as pltpu
from jax.sharding import PartitionSpec as P

HD = 128
TILE = 32
PER_ROW = 4
PER_LAYER = 16
LAYER = PER_LAYER * TILE
AXES = ("tile", "hid")
F32 = jnp.float32
BF16 = jnp.bfloat16


def route(move):
    pairs = []
    for x in range(4):
        for yl in range(2):
            for yh in range(2):
                for z in range(4):
                    for c in range(2):
                        a, b, d, e, f = move(x, yl, yh, z, c)
                        source = (yh * 8 + z * 2 + c) * 8 + x * 2 + yl
                        target = (d * 8 + e % 4 * 2 + f) * 8 + a % 4 * 2 + b
                        pairs.append((source, target))
    return pairs


def way(c):
    return 1 - 2 * c


X_A = route(lambda x, yl, yh, z, c: (x + way(c), yl, yh, z, c))
X_B = route(lambda x, yl, yh, z, c: (x - way(c), yl, yh, z, c))
X_1 = route(lambda x, yl, yh, z, c: (x ^ 1, yl, yh, z, c))
X_2 = route(lambda x, yl, yh, z, c: (x + 2, yl, yh, z, c))
Z_A = route(lambda x, yl, yh, z, c: (x, yl, yh, z + way(c), c))
Z_B = route(lambda x, yl, yh, z, c: (x, yl, yh, z - way(c), c))
Y_LO = route(lambda x, yl, yh, z, c: (x, 1 - yl, yh, z, c))
Y_HI = route(lambda x, yl, yh, z, c: (x, yl, 1 - yh, z, c))
CORE = route(lambda x, yl, yh, z, c: (x, yl, yh, z, 1 - c))
SWAP = route(lambda x, yl, yh, z, c: ((yh * 4 + z) // 2, z % 2, (x * 2 + yl) // 4, (x * 2 + yl) % 4, c))
NEXT = [(t * 8 + h, t * 8 + 8 + h) for t in range(15) for h in range(8)]
PREV = [(t * 8 + 8 + h, t * 8 + h) for t in range(15) for h in range(8)]


def send(array, pairs):
    return lax.ppermute(array, AXES, pairs)


def after(array, *others):
    return lax.optimization_barrier((array, *others))[0]


def start_weights(table, first, per, own, other, w_all, sems, depth):
    half = depth // 2
    for i in range(8):
        for part, refs_of in enumerate((own, other)):
            place = table[first[part] + i]
            target = w_all.at[pl.ds(i * depth + part * half, half), :]
            if len(refs_of) == 1:
                pltpu.make_async_copy(refs_of[0].at[place], target, sems.at[i]).start()
            else:

                @pl.when(place < per)
                def _():
                    source = refs_of[0].at[jnp.minimum(place, per - 1)]
                    pltpu.make_async_copy(source, target, sems.at[i]).start()

                @pl.when(place >= per)
                def _():
                    source = refs_of[1].at[jnp.maximum(place - per, 0)]
                    pltpu.make_async_copy(source, target, sems.at[i]).start()


def wait_weights(own, w_all, sems, depth, i):
    half = depth // 2
    for part in range(2):
        target = w_all.at[pl.ds(i * depth + part * half, half), :]
        pltpu.make_async_copy(own[0].at[0], target, sems.at[i]).wait()


PIECES = ((0, 1), (1, 2), (2, 4), (4, 6), (6, 8))
VMEM_BYTES = 60 * 2**20


def key_value_kernel(per, table, *refs):
    blocks, own, other = refs[:8], refs[8:10], refs[10:12]
    gain_ref, move_ref, x_out, out_ref, raw, x_all, w_all, x_sems, w_sems, out_sem = refs[12:]
    rows, depth = blocks[0].shape
    half = depth // 2
    core = table[16]
    for i in range(8):
        pltpu.make_async_copy(blocks[i], raw.at[i], x_sems.at[i]).start()
    start_weights(table, (8, 24), per, own, other, w_all, w_sems, depth)
    total = jnp.zeros((rows, 1), F32)
    for i in range(8):
        pltpu.make_async_copy(blocks[i], raw.at[i], x_sems.at[i]).wait()
        total += jnp.sum(raw[i].astype(F32), axis=1, keepdims=True)
    centre = total / (8 * depth)
    spread = jnp.zeros((rows, 1), F32)
    for i in range(8):
        spread += jnp.sum(jnp.square(raw[i].astype(F32) - centre), axis=1, keepdims=True)
    scale = lax.rsqrt(spread / (8 * depth) + 1e-06)
    total = None
    for lo, hi in PIECES:
        for i in range(lo, hi):
            for part, place in ((0, core), (1, 1 - core)):
                cols = pl.ds(pl.multiple_of(place * half, 128), half)
                value = (raw[i, :, cols].astype(F32) - centre) * scale
                value = value * (1.0 + gain_ref[table[i], :, cols]) + move_ref[table[i], :, cols]
                x_all[:, i * depth + part * half : i * depth + (part + 1) * half] = value.astype(BF16)
        for i in range(lo, hi):
            wait_weights(own, w_all, w_sems, depth, i)
        span = slice(lo * depth, hi * depth)
        prod = jnp.dot(x_all[:, span], w_all[span, :], preferred_element_type=F32)
        total = prod if total is None else total + prod
    copy = pltpu.make_async_copy(x_all, x_out, out_sem)
    copy.start()
    out_ref[...] = total.astype(BF16)
    copy.wait()


def key_value_rows(blocks, own_parts, other_parts, table, gains, moves):
    rows, depth = blocks[0].shape
    cols = own_parts[0].shape[2]
    vmem = pl.BlockSpec(memory_space=pltpu.VMEM)
    return pl.pallas_call(
        functools.partial(key_value_kernel, own_parts[0].shape[0]),
        in_specs=[pl.BlockSpec(memory_space=pltpu.SMEM)]
        + [pl.BlockSpec(memory_space=pl.ANY)] * 12
        + [vmem] * 2,
        out_specs=[pl.BlockSpec(memory_space=pl.ANY), vmem],
        out_shape=[
            jax.ShapeDtypeStruct((rows, 8 * depth), BF16),
            jax.ShapeDtypeStruct((rows, cols), BF16),
        ],
        scratch_shapes=[
            pltpu.VMEM((8, rows, depth), BF16),
            pltpu.VMEM((rows, 8 * depth), BF16),
            pltpu.VMEM((8 * depth, cols), BF16),
            pltpu.SemaphoreType.DMA((8,)),
            pltpu.SemaphoreType.DMA((8,)),
            pltpu.SemaphoreType.DMA,
        ],
        compiler_params=pltpu.CompilerParams(vmem_limit_bytes=VMEM_BYTES),
        name="key_value_rows",
    )(table, *blocks, *own_parts, *other_parts, gains, moves)


def query_kernel(table, x_ref, own, other, out_ref, x_all, w_all, x_sems, w_sems):
    depth = x_ref.shape[1] // 8
    start_weights(table, (0, 0), 8, [own], [other], w_all, w_sems, depth)

    def x_copy(i):
        cols = pl.ds(i * depth, depth)
        return pltpu.make_async_copy(x_ref.at[:, cols], x_all.at[:, cols], x_sems.at[i])

    for i in range(8):
        x_copy(i).start()
    total = None
    for lo, hi in PIECES:
        for i in range(lo, hi):
            wait_weights([own], w_all, w_sems, depth, i)
            x_copy(i).wait()
        span = slice(lo * depth, hi * depth)
        prod = jnp.dot(x_all[:, span], w_all[span, :], preferred_element_type=F32)
        total = prod if total is None else total + prod
    out_ref[...] = total.astype(BF16)


def query_rows(x_all, own, other, table):
    rows, width = x_all.shape
    cols = own.shape[2]
    return pl.pallas_call(
        query_kernel,
        in_specs=[pl.BlockSpec(memory_space=pltpu.SMEM)] + [pl.BlockSpec(memory_space=pl.ANY)] * 3,
        out_specs=pl.BlockSpec(memory_space=pltpu.VMEM),
        out_shape=jax.ShapeDtypeStruct((rows, cols), BF16),
        scratch_shapes=[
            pltpu.VMEM((rows, width), BF16),
            pltpu.VMEM((width, cols), BF16),
            pltpu.SemaphoreType.DMA((8,)),
            pltpu.SemaphoreType.DMA((8,)),
        ],
        compiler_params=pltpu.CompilerParams(vmem_limit_bytes=VMEM_BYTES),
        name="query_rows",
    )(table, x_all, own, other)


def attend_kernel(heads, *refs):
    sources, (out_ref, q_ref, prev_ref, own_ref, next_ref, bias_ref, sems) = refs[:5], refs[5:]
    copies = [
        pltpu.make_async_copy(source, target, sems.at[i])
        for i, (source, target) in enumerate(zip(sources, (q_ref, prev_ref, own_ref, next_ref, bias_ref)))
    ]
    for copy in copies:
        copy.start()
    for copy in copies:
        copy.wait()
    width = heads * HD
    row_len = PER_ROW * TILE
    for head in range(heads):
        cols = slice(head * HD, (head + 1) * HD)
        v_cols = slice(width + head * HD, width + (head + 1) * HD)
        for row in range(PER_LAYER // PER_ROW):
            lo = max(row - 1, 0) * row_len
            hi = min(row + 2, PER_LAYER // PER_ROW) * row_len
            queries = q_ref[row * row_len : (row + 1) * row_len, cols]
            scores = []
            for block, ref in enumerate((prev_ref, own_ref, next_ref)):
                part = lax.dot_general(
                    queries,
                    ref[lo:hi, cols],
                    (((1,), (1,)), ((), ())),
                    preferred_element_type=F32,
                ) * HD ** (-0.5)
                tiles = bias_ref[row * PER_ROW : (row + 1) * PER_ROW, block * LAYER + lo : block * LAYER + hi]
                part = part.reshape(PER_ROW, TILE, hi - lo) + tiles[:, None, :]
                scores.append(part.reshape(row_len, hi - lo))
            peak = functools.reduce(
                jnp.maximum, [jnp.max(part, axis=1, keepdims=True) for part in scores]
            )
            chances = [jnp.exp(part - peak) for part in scores]
            denom = sum(jnp.sum(part, axis=1, keepdims=True) for part in chances)
            total = sum(
                jnp.dot(part.astype(BF16), ref[lo:hi, v_cols], preferred_element_type=F32)
                for part, ref in zip(chances, (prev_ref, own_ref, next_ref))
            )
            out_ref[row * row_len : (row + 1) * row_len, cols] = (total / denom).astype(BF16)


def attend(*arrays):
    queries = arrays[0]
    heads = queries.shape[1] // HD
    return pl.pallas_call(
        functools.partial(attend_kernel, heads),
        in_specs=[pl.BlockSpec(memory_space=pl.ANY)] * 5,
        out_specs=pl.BlockSpec(memory_space=pltpu.VMEM),
        out_shape=jax.ShapeDtypeStruct(queries.shape, BF16),
        scratch_shapes=[pltpu.VMEM(array.shape, array.dtype) for array in arrays]
        + [pltpu.SemaphoreType.DMA((5,))],
        compiler_params=pltpu.CompilerParams(vmem_limit_bytes=VMEM_BYTES),
        name="attend",
    )(*arrays)


def output_kernel(first, count, last, table, *refs):
    parts, (own, other), rest = refs[:count], refs[count : count + 2], refs[count + 2 :]
    if last:
        sum_ref, res_ref, gate_ref, out_ref, x_all, w_all, sems = rest
    else:
        out_ref, x_all, w_all, sems = rest
    core = table[16]
    depth, half = own.shape[1:]

    def pairs(i):
        yield parts[i], x_all.at[:, pl.ds(i * depth, depth)]
        for ref, place in ((own, core), (other, 1 - core)):
            cols = pl.ds(pl.multiple_of(place * half, 128), half)
            yield ref.at[table[first + i]], w_all.at[pl.ds(i * depth, depth), cols]

    for i in range(count):
        for source, target in pairs(i):
            pltpu.make_async_copy(source, target, sems.at[i]).start()
    total = sum_ref[...] if last else None
    for lo in range(0, count, 2):
        hi = min(lo + 2, count)
        for i in range(lo, hi):
            for source, target in pairs(i):
                pltpu.make_async_copy(source, target, sems.at[i]).wait()
        span = slice(lo * depth, hi * depth)
        prod = jnp.dot(x_all[:, span], w_all[span, :], preferred_element_type=F32)
        total = prod if total is None else total + prod
    if last:
        total = res_ref[...].astype(F32) + gate_ref[...] * total
    out_ref[...] = total.astype(out_ref.dtype)


def output_rows(parts, first, own, other, table, last=()):
    count = len(parts)
    rows = parts[0].shape[0]
    depth = own.shape[1]
    cols = 2 * own.shape[2]
    vmem = pl.BlockSpec(memory_space=pltpu.VMEM)
    return pl.pallas_call(
        functools.partial(output_kernel, first, count, bool(last)),
        in_specs=[pl.BlockSpec(memory_space=pltpu.SMEM)]
        + [pl.BlockSpec(memory_space=pl.ANY)] * (count + 2)
        + [vmem] * len(last),
        out_specs=vmem,
        out_shape=jax.ShapeDtypeStruct((rows, cols), BF16 if last else F32),
        scratch_shapes=[
            pltpu.VMEM((rows, count * depth), BF16),
            pltpu.VMEM((count * depth, cols), BF16),
            pltpu.SemaphoreType.DMA((count,)),
        ],
        compiler_params=pltpu.CompilerParams(vmem_limit_bytes=VMEM_BYTES),
        name="output_rows",
    )(table, *parts, own, other, *last)


def stack_kernel(places, *refs):
    blocks, out_ref, sems = refs[:-2], refs[-2], refs[-1]
    copies = []
    for block, (source, target) in zip(blocks, places):
        source = block if source is None else block.at[source]
        target = out_ref.at[target[0], pl.ds(target[1], source.shape[0])]
        copies.append(pltpu.make_async_copy(source, target, sems.at[len(copies)]))
    for copy in copies:
        copy.start()
    for copy in copies:
        copy.wait()


def stack(blocks, places, shape):
    return pl.pallas_call(
        functools.partial(stack_kernel, places),
        in_specs=[pl.BlockSpec(memory_space=pl.ANY)] * len(blocks),
        out_specs=pl.BlockSpec(memory_space=pltpu.VMEM),
        out_shape=jax.ShapeDtypeStruct(shape, blocks[0].dtype),
        scratch_shapes=[pltpu.SemaphoreType.DMA((len(blocks),))],
        name="stack",
    )(*blocks)


def places():
    rows = np.zeros((128, 32), np.int32)
    for tile in range(16):
        for hid in range(8):
            x, yl, yh, z, c = hid // 2, hid % 2, tile // 8, tile // 2 % 4, tile % 2
            row = rows[tile * 8 + hid]
            row[:8] = [(x + s) % 4 * 2 + (yl ^ k) for k in range(2) for s in (0, -way(c), way(c), 2)]
            for first, w in ((8, way(c)), (24, -way(c))):
                pairs = [(yh ^ k) * 4 + (z + s) % 4 for k in range(2) for s in (0, -w, w, 2)]
                pairs = [pairs[i] for i in (0, 1, 2, 4, 5, 6, 3, 7)]
                row[first : first + 8] = [pairs.index(hid_of) for hid_of in row[:8]]
            row[16] = c
    return rows


def body(
    residual_in, w_query, w_key, w_value, w_output, shift_mod, scale_mod, gate_mod, neighbours
):
    tok_rows, feat_cols = residual_in.shape
    tile_id, hid_id = lax.axis_index("tile"), lax.axis_index("hid")
    table = lax.dynamic_index_in_dim(jnp.asarray(places()), tile_id * 8 + hid_id, 0, keepdims=False)
    pair_groups = [[p * 2 + c for p in range(8)] for c in range(2)]

    w_kv = jnp.concatenate([w_key, w_value], axis=1)
    w_rows, w_cols = w_kv.shape
    w_half = w_rows // 2
    x_a, x_b, w_a, w_b, w_mate, own, w_kv, w_q = lax.optimization_barrier(
        (
            send(residual_in, X_A),
            send(residual_in, X_B),
            send(w_kv, Z_A),
            send(w_kv, Z_B),
            send(w_kv, Y_HI),
            residual_in,
            w_kv,
            w_query,
        )
    )

    q_own = lax.all_gather(w_q[None], "tile", axis=0, axis_index_groups=pair_groups, tiled=True)
    early = stack([w_kv, w_a, w_b, w_mate], [(None, (i, 0)) for i in range(4)], (4, w_rows, w_cols))
    far, mate, w_mate_a, w_mate_b, early_other, x_a, x_b, w_a, w_b, own, early = (
        lax.optimization_barrier(
            (
                send(own, X_2),
                send(own, Y_LO),
                send(w_mate, Z_A),
                send(w_mate, Z_B),
                send(early, CORE),
                x_a,
                x_b,
                w_a,
                w_b,
                own,
                early,
            )
        )
    )

    mate_a = send(mate, X_A)
    mate_b = send(mate, X_B)
    mate_far = send(far, Y_LO)
    w_fwd_a = send(jnp.stack([w_a[:w_half], w_mate_a[:w_half]]), Z_A)
    w_fwd_b = send(jnp.stack([w_b[w_half:], w_mate_b[w_half:]]), Z_B)
    late = stack(
        [w_mate_a, w_mate_b, w_fwd_a, w_fwd_b, w_fwd_a, w_fwd_b],
        [(None, (0, 0)), (None, (1, 0)), (0, (2, 0)), (0, (2, w_half)), (1, (3, 0)), (1, (3, w_half))],
        (4, w_rows, w_cols),
    )
    late_other = send(late, CORE)
    mate_a, mate_b, mate_far, late, late_other, w_o = lax.optimization_barrier(
        (mate_a, mate_b, mate_far, late, late_other, w_output)
    )
    q_other = send(after(q_own, late_other), CORE)
    o_block = send(w_o, SWAP)

    listed = (neighbours >= 0).reshape(PER_LAYER, 3, 3, 3)
    grid = np.arange(PER_LAYER)
    row_step = grid[None, :] // PER_ROW - grid[:, None] // PER_ROW
    col_step = grid[None, :] % PER_ROW - grid[:, None] % PER_ROW
    bias = jnp.full((PER_LAYER, 3, PER_LAYER), -1e30, F32)
    for b in range(-1, 2):
        for e in range(-1, 2):
            here = jnp.asarray((row_step == b) & (col_step == e))[:, None, :]
            bias = jnp.where(here & listed[:, :, b + 1, e + 1][:, :, None], 0.0, bias)
    bias = jnp.repeat(bias.reshape(PER_LAYER, 3 * PER_LAYER), TILE, axis=1)

    x_all, key_value = key_value_rows(
        [own, x_a, x_b, far, mate, mate_a, mate_b, mate_far],
        [early, late],
        [early_other, late_other],
        table,
        scale_mod.reshape(8, 1, feat_cols),
        shift_mod.reshape(8, 1, feat_cols),
    )
    x_all, key_value, o_block = lax.optimization_barrier((x_all, key_value, o_block))
    o_own = lax.all_gather(o_block[None], "tile", axis=0, axis_index_groups=pair_groups, tiled=True)
    queries = query_rows(x_all, q_own, q_other, table)
    before, later, queries, key_value = lax.optimization_barrier(
        (send(key_value, NEXT), send(key_value, PREV), queries, key_value)
    )
    pieces = attend(queries, before, key_value, later, bias)

    p_a, p_b, p_far, p_mate, pieces = lax.optimization_barrier(
        (send(pieces, X_A), send(pieces, X_B), send(pieces, X_2), send(pieces, Y_LO), pieces)
    )
    o_other = send(after(o_own, p_a), CORE)
    p_mate_a = send(p_mate, X_A)
    p_mate_b = send(p_mate, X_B)
    p_mate_far = send(p_far, Y_LO)
    first = output_rows([pieces, p_a, p_b, p_far, p_mate], 0, o_own, o_other, table)
    gate = lax.dynamic_slice_in_dim(gate_mod, hid_id * feat_cols, feat_cols)[None]
    last = (first, residual_in, gate)
    return output_rows([p_mate_a, p_mate_b, p_mate_far], 5, o_own, o_other, table, last)


def solution(mesh):
    placed = (
        P("tile", "hid"),
        P("tile", "hid"),
        P("tile", "hid"),
        P("tile", "hid"),
        P("hid", "tile"),
        P(),
        P(),
        P(),
        P("tile", None),
    )
    return jax.shard_map(
        body, mesh=mesh, in_specs=placed, out_specs=P("tile", "hid"), check_vma=False
    )
```

time: 530 us -> 231 us (0.44)
  waiting for transfers between devices: 438 us -> 92.9 us
  Pallas kernels: 0 us -> 54.1 us
  starting transfers between devices: 4.73 us -> 52.1 us
  matrix products: 34.9 us -> 0 us
  other arithmetic: 20.8 us -> 1.12 us
    all_gather x5 -> x2, waiting for transfers between devices: 308 us -> 10.3 us  [the longest x1 10.2 us: body(): lax.all_gather(o_block[None], 'tile', axis=0, axis_index_groups=pair_grou...]
    reduce_scatter x1 -> x0, waiting for transfers between devices: 126 us -> none  [body(): lax.psum_scatter(partial_out.astype(jnp.bfloat16), 'hid', scatter_dimensi...]
    ppermute x2 -> x28, waiting for transfers between devices: 0.01 us -> 82.6 us  [send(): return lax.ppermute(array, AXES, pairs)]
    pallas_call x0 -> x7, Pallas kernels: none -> 54.1 us  [the longest x1 22.1 us: key_value_rows(): pl.pallas_call(functools.partial(key_value_kernel, own_parts[0].shape[0])...]
    ppermute x2 -> x28, starting transfers between devices: 4.54 us -> 52.1 us  [send(): return lax.ppermute(array, AXES, pairs)]
    dot_general x6 -> x0, matrix products: 34.9 us -> none  [the longest x1 7.77 us: body(): jnp.dot(pieces_out, lax.all_gather(w_output, 'tile', axis=1, tiled=True),...]
    broadcast_in_dim x2, local copies, waits for them, and re-layouts: 10.4 us -> 0.75 us  [the longest x1 0.6 us: body(): lax.dynamic_slice_in_dim(gate_mod, hid_id * feat_cols, feat_cols)[None]]
    convert_element_type x2 -> x0, other arithmetic: 8.56 us -> none  [the longest x1 6.31 us: body(): modded = (normed * (1.0 + scale_mod) + shift_mod).astype(jnp.bfloat16)]
  transfers between devices with their start and end apart: 8 -> 30, of which waited for: 6 -> 16; matrix products, arithmetic and copies ran while one was open for 12% -> 4% of each run, Pallas kernels for 0% -> 20%
where the time goes in v1:
time: 231 us; the launch traced here: 230 us
  waiting for transfers between devices  92.9 us (40%)
  Pallas kernels  54.1 us (23%)
  starting transfers between devices  52.1 us (23%)
  local copies, waits for them, and re-layouts  16.1 us (7%)
  between operations  13.7 us (6%)
    ppermute x28, waiting for transfers between devices, send(): return lax.ppermute(array, AXES, pairs)  82.6 us
    ppermute x28, starting transfers between devices, send(): return lax.ppermute(array, AXES, pairs)  52.1 us
    pallas_call x1, Pallas kernels, key_value_rows(): pl.pallas_call(functools.partial(key_value_kernel, own_parts[0].shape[0])...  22.1 us
    pallas_call x2, Pallas kernels, output_rows(): pl.pallas_call(functools.partial(output_kernel, first, count, bool(last))...  11.5 us
    all_gather x1, waiting for transfers between devices, body(): lax.all_gather(o_block[None], 'tile', axis=0, axis_index_groups=pair_grou...  10.2 us
    unnamed x47, local copies, waits for them, and re-layouts  7.9 us
    pallas_call x1, Pallas kernels, query_rows(): pl.pallas_call(query_kernel, in_specs=[pl.BlockSpec(memory_space=pltpu.SM...  7.4 us
    pallas_call x1, Pallas kernels, attend(): pl.pallas_call(functools.partial(attend_kernel, heads), in_specs=[pl.Bloc...  7.01 us
  transfers between devices with their start and end apart: 30, of which 16 were waited for; matrix products, arithmetic and copies ran while one was open for 4% of the time, Pallas kernels for 20%

profile of v1, /device:TPU:1, one launch (start us, length us, event | category | flops | bytes accessed | tf_op | source)
XLA Modules:
  0.0 230.2 jit_solution(13466176605042063446)
XLA Ops:
  6.5 3.3 %collective-permute-start = (bf16[512,768]{1,0:T(8,128)(2,1)}, bf16[512,768]{1,0:T(8,128)(2,1)}, u32[]{:S(2)}, u32[]{:S(2)}) collective-permute-start(bf16[512,768]{1,0:T(8,128)(2,1)} %refs_6_.1), channel_id=1, source_target_pairs={{0,2},{8,14},{16,18},{24,30},{32,34},{40,46},{48,50},{56,62},{64,6... | collective-permute-start | bytes 2359304 | tf_op jit(solution)/shard_map/ppermute | solution.py:54
  9.8 1.0 constant_dynamic-update-slice_fusion.1
  10.8 1.0 constant_dynamic-update-slice_fusion.refs_0_
  11.9 3.8 %collective-permute-start.2 = (bf16[384,768]{1,0:T(8,128)(2,1)S(1)}, bf16[384,768]{1,0:T(8,128)(2,1)S(1)}, u32[]{:S(2)}, u32[]{:S(2)}) collective-permute-start(bf16[384,768]{1,0:T(8,128)(2,1)S(1)} %constant_dynamic-update-slice_fusion.refs_0_), channel_id=1, source_target_pairs={{0,16},{8,56},{16,32},{24,8},{32,48},{40,24},{48,0},{56,40},{64,80... | collective-permute-start | bytes 1769480 | tf_op jit(solution)/shard_map/ppermute | solution.py:54
  15.7 2.9 %collective-permute-start.4 = (bf16[384,768]{1,0:T(8,128)(2,1)S(1)}, bf16[384,768]{1,0:T(8,128)(2,1)S(1)}, u32[]{:S(2)}, u32[]{:S(2)}) collective-permute-start(bf16[384,768]{1,0:T(8,128)(2,1)S(1)} %constant_dynamic-update-slice_fusion.refs_0_), channel_id=1, source_target_pairs={{0,64},{8,72},{16,80},{24,88},{32,96},{40,104},{48,112},{56,120},{... | collective-permute-start | bytes 1769480 | tf_op jit(solution)/shard_map/ppermute | solution.py:54
  18.6 8.2 %collective-permute-done.2.refs_1_ = bf16[384,768]{1,0:T(8,128)(2,1)S(1)} collective-permute-done((bf16[384,768]{1,0:T(8,128)(2,1)S(1)}, bf16[384,768]{1,0:T(8,128)(2,1)S(1)}, u32[]{:S(2)}, u32[]{:S(2)}) %collective-permute-start.2) | collective-permute-done | bytes 589856 | tf_op jit(solution)/shard_map/ppermute | solution.py:54
  26.8 4.4 %collective-permute-done.3.refs_2_ = bf16[384,768]{1,0:T(8,128)(2,1)S(1)} collective-permute-done((bf16[384,768]{1,0:T(8,128)(2,1)S(1)}, bf16[384,768]{1,0:T(8,128)(2,1)S(1)}, u32[]{:S(2)}, u32[]{:S(2)}) %collective-permute-start.3) | collective-permute-done | bytes 589856 | tf_op jit(solution)/shard_map/ppermute | solution.py:54
  31.3 0.8 copy-done.10
  32.0 0.2 copy-done.15
  32.2 3.0 %stack.26.refs_8_ = bf16[4,384,768]{2,1,0:T(8,128)(2,1)} custom-call(bf16[384,768]{1,0:T(8,128)(2,1)} %copy-done.7, bf16[384,768]{1,0:T(8,128)(2,1)} %copy-done.8, bf16[384,768]{1,0:T(8,128)(2,1)} %copy-done.10, bf16[384,768]{1,0:T(8,128)(2,1)} %copy-done.15), custom_call_target="tpu_custom_call" | custom-call | tf_op jit(solution)/shard_map/stack/pallas_call | solution.py:323
  35.3 1.6 collective-permute-start.9
  36.9 1.7 collective-permute-start.5
  38.7 1.3 collective-permute-start.6
  40.0 2.7 %collective-permute-start.7 = (bf16[384,768]{1,0:T(8,128)(2,1)}, bf16[384,768]{1,0:T(8,128)(2,1)}, u32[]{:S(2)}, u32[]{:S(2)}) collective-permute-start(bf16[384,768]{1,0:T(8,128)(2,1)} %copy-done.15), channel_id=1, source_target_pairs={{0,16},{8,56},{16,32},{24,8},{32,48},{40,24},{48,0},{56,40},{64,80... | collective-permute-start | bytes 1769480 | tf_op jit(solution)/shard_map/ppermute | solution.py:54
  42.7 13.5 %collective-permute-done.7.refs_0_ = bf16[384,768]{1,0:T(8,128)(2,1)} collective-permute-done((bf16[384,768]{1,0:T(8,128)(2,1)}, bf16[384,768]{1,0:T(8,128)(2,1)}, u32[]{:S(2)}, u32[]{:S(2)}) %collective-permute-start.7) | collective-permute-done | bytes 589856 | tf_op jit(solution)/shard_map/ppermute | solution.py:54
  56.3 3.3 %collective-permute-done.8.refs_1_ = bf16[384,768]{1,0:T(8,128)(2,1)} collective-permute-done((bf16[384,768]{1,0:T(8,128)(2,1)}, bf16[384,768]{1,0:T(8,128)(2,1)}, u32[]{:S(2)}, u32[]{:S(2)}) %collective-permute-start.8) | collective-permute-done | bytes 589856 | tf_op jit(solution)/shard_map/ppermute | solution.py:54
  59.5 0.6 collective-permute-done.6.refs_4_
  60.1 1.5 slice_bitcast_fusion
  61.8 1.0 slice_bitcast_fusion.2
  62.9 2.7 %collective-permute-start.13 = (bf16[2,192,768]{2,1,0:T(8,128)(2,1)S(1)}, bf16[2,192,768]{2,1,0:T(8,128)(2,1)S(1)}, u32[]{:S(2)}, u32[]{:S(2)}) collective-permute-start(bf16[2,192,768]{2,1,0:T(8,128)(2,1)S(1)} %pad_maximum_fusion), channel_id=1, source_target_pairs={{0,16},{8,56},{16,32},{24,8},{32,48},{40,24},{48,0},{56,40},{64,80... | collective-permute-start | bytes 1769480 | tf_op jit(solution)/shard_map/ppermute | solution.py:54
  65.6 10.7 %collective-permute-done.14.refs_3_.refs_5_ = bf16[2,192,768]{2,1,0:T(8,128)(2,1)S(1)} collective-permute-done((bf16[2,192,768]{2,1,0:T(8,128)(2,1)S(1)}, bf16[2,192,768]{2,1,0:T(8,128)(2,1)S(1)}, u32[]{:S(2)}, u32[]{:S(2)}) %collective-permute-start.14) | collective-permute-done | bytes 589856 | tf_op jit(solution)/shard_map/ppermute | solution.py:54
  76.3 4.3 %collective-permute-done.13.refs_2_.refs_4_ = bf16[2,192,768]{2,1,0:T(8,128)(2,1)S(1)} collective-permute-done((bf16[2,192,768]{2,1,0:T(8,128)(2,1)S(1)}, bf16[2,192,768]{2,1,0:T(8,128)(2,1)S(1)}, u32[]{:S(2)}, u32[]{:S(2)}) %collective-permute-start.13) | collective-permute-done | bytes 589856 | tf_op jit(solution)/shard_map/ppermute | solution.py:54
  80.6 0.8 copy-done.3
  81.5 3.1 %stack.27.refs_9_ = bf16[4,384,768]{2,1,0:T(8,128)(2,1)} custom-call(bf16[384,768]{1,0:T(8,128)(2,1)} %collective-permute-done.7.refs_0_, bf16[384,768]{1,0:T(8,128)(2,1)} %collective-permute-done.8.refs_1_, bf16[2,192,768]{2,1,0:T(8,128)(2,1)} %copy-done.3, bf16[2,192,768]{2,1,0:T(8,128)(2,1)} %copy-done.2, bf16[2,192,768]{2,1,0:T(8,128)(2,1)} %copy-done.3, ...), custom_call_target="tpu_custom_call" | custom-call | tf_op jit(solution)/shard_map/stack/pallas_call | solution.py:323
  84.5 3.6 %collective-permute-start.15 = (bf16[4,384,768]{2,1,0:T(8,128)(2,1)}, bf16[4,384,768]{2,1,0:T(8,128)(2,1)S(1)}, u32[]{:S(2)}, u32[]{:S(2)}) collective-permute-start(bf16[4,384,768]{2,1,0:T(8,128)(2,1)} %stack.27.refs_9_), channel_id=1, source_target_pairs={{0,8},{8,0},{16,24},{24,16},{32,40},{40,32},{48,56},{56,48},{64,72... | collective-permute-start | bytes 7077896 | tf_op jit(solution)/shard_map/ppermute | solution.py:54
  88.1 1.5 collective-permute-start.11
  89.6 0.9 collective-permute-start.12
  90.4 15.2 %collective-permute-done.10.refs_5_ = bf16[512,768]{1,0:T(8,128)(2,1)S(1)} collective-permute-done((bf16[512,768]{1,0:T(8,128)(2,1)}, bf16[512,768]{1,0:T(8,128)(2,1)S(1)}, u32[]{:S(2)}, u32[]{:S(2)}) %collective-permute-start.10) | collective-permute-done | bytes 786464 | tf_op jit(solution)/shard_map/ppermute | solution.py:54
  105.6 3.0 %collective-permute-done.11.refs_6_ = bf16[512,768]{1,0:T(8,128)(2,1)S(1)} collective-permute-done((bf16[512,768]{1,0:T(8,128)(2,1)}, bf16[512,768]{1,0:T(8,128)(2,1)S(1)}, u32[]{:S(2)}, u32[]{:S(2)}) %collective-permute-start.11) | collective-permute-done | bytes 786464 | tf_op jit(solution)/shard_map/ppermute | solution.py:54
  108.7 0.9 copy-done.12
  109.5 1.8 collective-permute-start.16
  111.3 1.3 dynamic-slice_bitcast_fusion.table
  112.6 22.1 %key_value_rows.1 = (bf16[512,6144]{1,0:T(8,128)(2,1)}, bf16[512,768]{1,0:T(8,128)(2,1)}) custom-call(s32[32]{0:T(128)} %dynamic-slice_bitcast_fusion.table, bf16[512,768]{1,0:T(8,128)(2,1)} %refs_6_.1, bf16[512,768]{1,0:T(8,128)(2,1)} %collective-permute-done.refs_1_, bf16[512,768]{1,0:T(8,128)(2,1)} %collective-permute-done.1.refs_2_, ...), custom_call_target="tpu_custom_call" | custom-call | tf_op jit(solution)/shard_map/key_value_rows/pallas_call | solution.py:134
  134.7 0.7 copy-done.19
  135.5 1.0 collective-permute-start.19
  136.5 4.5 %collective-permute-start.17 = (bf16[512,768]{1,0:T(8,128)(2,1)}, bf16[512,768]{1,0:T(8,128)(2,1)S(1)}, u32[]{:S(2)}, u32[]{:S(2)}) collective-permute-start(bf16[512,768]{1,0:T(8,128)(2,1)} %get-tuple-element.78.refs_2_), channel_id=1, source_target_pairs={{0,8},{1,9},{2,10},{3,11},{4,12},{5,13},{6,14},{7,15},{8,16},{9,17... | collective-permute-start | bytes 2359304 | tf_op jit(solution)/shard_map/ppermute | solution.py:54
  140.9 1.9 collective-permute-start.18
  142.9 0.1 copy.48
  143.0 0.1 copy.60
  143.1 0.1 copy.61
  143.9 1.0 select_select_fusion
  145.0 0.2 broadcast_in_dim.42
  145.2 0.8 reshape.68.refs_4_
  146.0 1.5 copy-done.5
  147.5 7.4 %query_rows.1.refs_0_ = bf16[512,384]{1,0:T(8,128)(2,1)} custom-call(s32[32]{0:T(128)} %dynamic-slice_bitcast_fusion.table, bf16[512,6144]{1,0:T(8,128)(2,1)} %get-tuple-element.73.x_ref, bf16[8,384,384]{2,1,0:T(8,128)(2,1)} %bitcast.29, bf16[8,384,384]{2,1,0:T(8,128)(2,1)} %copy-done.5), custom_call_target="tpu_custom_call" | custom-call | tf_op jit(solution)/shard_map/query_rows/pallas_call | solution.py:181
  154.9 0.3 collective-permute-done.18.refs_3_
  155.2 0.6 copy-done.14
  155.8 7.0 %attend.1.refs_0_ = bf16[512,384]{1,0:T(8,128)(2,1)} custom-call(bf16[512,384]{1,0:T(8,128)(2,1)} %query_rows.1.refs_0_, bf16[512,768]{1,0:T(8,128)(2,1)} %copy-done.14, bf16[512,768]{1,0:T(8,128)(2,1)} %get-tuple-element.78.refs_2_, bf16[512,768]{1,0:T(8,128)(2,1)} %collective-permute-done.18.refs_3_, f32[16,1536]{1,0:T(8,128)} %reshape.68.refs_4_), custom_call_target="tpu_custom_call" | custom-call | tf_op jit(solution)/shard_map/attend/pallas_call | solution.py:242
  162.8 12.2 %collective-permute-start.20 = (bf16[512,384]{1,0:T(8,128)(2,1)}, bf16[512,384]{1,0:T(8,128)(2,1)S(1)}, u32[]{:S(2)}, u32[]{:S(2)}) collective-permute-start(bf16[512,384]{1,0:T(8,128)(2,1)} %attend.1.refs_0_), channel_id=1, source_target_pairs={{0,2},{8,14},{16,18},{24,30},{32,34},{40,46},{48,50},{56,62},{64,6... | collective-permute-start | bytes 1179656 | tf_op jit(solution)/shard_map/ppermute | solution.py:54
  175.1 1.3 collective-permute-start.22
  176.3 13.7 %collective-permute-done.20.refs_1_ = bf16[512,384]{1,0:T(8,128)(2,1)S(1)} collective-permute-done((bf16[512,384]{1,0:T(8,128)(2,1)}, bf16[512,384]{1,0:T(8,128)(2,1)S(1)}, u32[]{:S(2)}, u32[]{:S(2)}) %collective-permute-start.20) | collective-permute-done | bytes 393248 | tf_op jit(solution)/shard_map/ppermute | solution.py:54
  190.0 1.9 collective-permute-done.22.refs_3_
  191.9 2.0 collective-permute-done.23.refs_4_
  193.9 10.2 %all-gather.7.cloned.1.call-done = bf16[3072,384]{1,0:T(8,128)(2,1)} async-done(((bf16[384,384]{1,0:T(8,128)(2,1)}), bf16[3072,384]{1,0:T(8,128)(2,1)}) %all-gather.7.cloned.1.call-update) | async-done | bytes 2359312 | tf_op jit(solution)/shard_map/all_gather | solution.py:429
  204.1 0.8 collective-permute-start.27
  204.9 2.4 %collective-permute-start.24 = (bf16[512,384]{1,0:T(8,128)(2,1)}, bf16[512,384]{1,0:T(8,128)(2,1)}, u32[]{:S(2)}, u32[]{:S(2)}) collective-permute-start(bf16[512,384]{1,0:T(8,128)(2,1)} %collective-permute-done.23.refs_4_), channel_id=1, source_target_pairs={{0,2},{8,14},{16,18},{24,30},{32,34},{40,46},{48,50},{56,62},{64,6... | collective-permute-start | bytes 1179656 | tf_op jit(solution)/shard_map/ppermute | solution.py:54
  207.3 0.2 collective-permute-start.26
  207.5 0.8 dynamic_slice.8
  208.2 0.6 broadcast_in_dim.44.refs_7_
  208.8 0.5 collective-permute-done.27.refs_6_.refs_4_
  209.3 1.4 copy-done
  210.7 6.0 %output_rows.2.refs_5_ = f32[512,768]{1,0:T(8,128)} custom-call(s32[32]{0:T(128)} %dynamic-slice_bitcast_fusion.table, bf16[512,384]{1,0:T(8,128)(2,1)} %attend.1.refs_0_, bf16[512,384]{1,0:T(8,128)(2,1)} %copy-done.17, bf16[512,384]{1,0:T(8,128)(2,1)} %copy-done.18, bf16[512,384]{1,0:T(8,128)(2,1)} %copy-done.16, ...), custom_call_target="tpu_custom_call" | custom-call | tf_op jit(solution)/shard_map/output_rows/pallas_call | solution.py:292
  216.7 1.0 collective-permute-done.25.refs_1_
  217.8 5.5 %output_rows.3 = bf16[512,768]{1,0:T(8,128)(2,1)} custom-call(s32[32]{0:T(128)} %dynamic-slice_bitcast_fusion.table, bf16[512,384]{1,0:T(8,128)(2,1)} %collective-permute-done.24.refs_0_, bf16[512,384]{1,0:T(8,128)(2,1)} %collective-permute-done.25.refs_1_, bf16[512,384]{1,0:T(8,128)(2,1)} %collective-permute-done.26.refs_2_, bf16[8,384,384]{2,1,0:T(8,128)(2,1)} %bitcast.27, ...), custom_call_target="tpu_custom_call" | custom-call | tf_op jit(solution)/shard_map/output_rows/pallas_call | solution.py:292
  (77 shorter events, 1.2 us)
Async XLA Ops:
  6.5 129.0 %all-gather.5.cloned.1.call-start = ((), (), s32[]{:S(2)}) async-start(), calls=%async_computation | async-start | bytes 2654208 | tf_op jit(solution)/shard_map/all_gather | solution.py:372
  6.5 24.7 %collective-permute-start = (bf16[512,768]{1,0:T(8,128)(2,1)}, bf16[512,768]{1,0:T(8,128)(2,1)}, u32[]{:S(2)}, u32[]{:S(2)}) collective-permute-start(bf16[512,768]{1,0:T(8,128)(2,1)} %refs_6_.1), channel_id=1, source_target_pairs={{0,2},{8,14},{16,18},{24,30},{32,34},{40,46},{48,50},{56,62},{64,6... | collective-permute-start | bytes 2359304 | tf_op jit(solution)/shard_map/ppermute | solution.py:54
  9.8 21.4 %collective-permute-start.1 = (bf16[512,768]{1,0:T(8,128)(2,1)}, bf16[512,768]{1,0:T(8,128)(2,1)}, u32[]{:S(2)}, u32[]{:S(2)}) collective-permute-start(bf16[512,768]{1,0:T(8,128)(2,1)} %refs_6_.1), channel_id=1, source_target_pairs={{0,6},{8,10},{16,22},{24,26},{32,38},{40,42},{48,54},{56,58},{64,7... | collective-permute-start | bytes 2359304 | tf_op jit(solution)/shard_map/ppermute | solution.py:54
  11.9 19.4 %copy-start.7 = (bf16[384,768]{1,0:T(8,128)(2,1)}, bf16[384,768]{1,0:T(8,128)(2,1)S(1)}, u32[]{:S(2)}) copy-start(bf16[384,768]{1,0:T(8,128)(2,1)S(1)} %constant_dynamic-update-slice_fusion.refs_0_) | copy-start | bytes 1769476
  11.9 25.0 %copy-start.1 = (bf16[512,768]{1,0:T(8,128)(2,1)S(1)}, bf16[512,768]{1,0:T(8,128)(2,1)}, u32[]{:S(2)}) copy-start(bf16[512,768]{1,0:T(8,128)(2,1)} %refs_6_.1) | copy-start | bytes 2359300
  11.9 14.9 %collective-permute-start.2 = (bf16[384,768]{1,0:T(8,128)(2,1)S(1)}, bf16[384,768]{1,0:T(8,128)(2,1)S(1)}, u32[]{:S(2)}, u32[]{:S(2)}) collective-permute-start(bf16[384,768]{1,0:T(8,128)(2,1)S(1)} %constant_dynamic-update-slice_fusion.refs_0_), channel_id=1, source_target_pairs={{0,16},{8,56},{16,32},{24,8},{32,48},{40,24},{48,0},{56,40},{64,80... | collective-permute-start | bytes 1769480 | tf_op jit(solution)/shard_map/ppermute | solution.py:54
  15.7 15.5 %collective-permute-start.3 = (bf16[384,768]{1,0:T(8,128)(2,1)S(1)}, bf16[384,768]{1,0:T(8,128)(2,1)S(1)}, u32[]{:S(2)}, u32[]{:S(2)}) collective-permute-start(bf16[384,768]{1,0:T(8,128)(2,1)S(1)} %constant_dynamic-update-slice_fusion.refs_0_), channel_id=1, source_target_pairs={{0,48},{8,24},{16,0},{24,40},{32,16},{40,56},{48,32},{56,8},{64,11... | collective-permute-start | bytes 1769480 | tf_op jit(solution)/shard_map/ppermute | solution.py:54
  15.7 15.5 %collective-permute-start.4 = (bf16[384,768]{1,0:T(8,128)(2,1)S(1)}, bf16[384,768]{1,0:T(8,128)(2,1)S(1)}, u32[]{:S(2)}, u32[]{:S(2)}) collective-permute-start(bf16[384,768]{1,0:T(8,128)(2,1)S(1)} %constant_dynamic-update-slice_fusion.refs_0_), channel_id=1, source_target_pairs={{0,64},{8,72},{16,80},{24,88},{32,96},{40,104},{48,112},{56,120},{... | collective-permute-start | bytes 1769480 | tf_op jit(solution)/shard_map/ppermute | solution.py:54
  26.8 4.4 %copy-start.8 = (bf16[384,768]{1,0:T(8,128)(2,1)}, bf16[384,768]{1,0:T(8,128)(2,1)S(1)}, u32[]{:S(2)}) copy-start(bf16[384,768]{1,0:T(8,128)(2,1)S(1)} %collective-permute-done.2.refs_1_) | copy-start | bytes 1769476
  31.2 0.8 copy-start.10
  31.2 1.0 copy-start.15
  35.3 24.9 %collective-permute-start.9 = (bf16[4,384,768]{2,1,0:T(8,128)(2,1)}, bf16[4,384,768]{2,1,0:T(8,128)(2,1)S(1)}, u32[]{:S(2)}, u32[]{:S(2)}) collective-permute-start(bf16[4,384,768]{2,1,0:T(8,128)(2,1)} %stack.26.refs_8_), channel_id=1, source_target_pairs={{0,8},{8,0},{16,24},{24,16},{32,40},{40,32},{48,56},{56,48},{64,72... | collective-permute-start | bytes 7077896 | tf_op jit(solution)/shard_map/ppermute | solution.py:54
  36.9 22.6 %collective-permute-start.5 = (bf16[512,768]{1,0:T(8,128)(2,1)S(1)}, bf16[512,768]{1,0:T(8,128)(2,1)}, u32[]{:S(2)}, u32[]{:S(2)}) collective-permute-start(bf16[512,768]{1,0:T(8,128)(2,1)S(1)} %copy-done.1), channel_id=1, source_target_pairs={{0,4},{8,12},{16,20},{24,28},{32,36},{40,44},{48,52},{56,60},{64,6... | collective-permute-start | bytes 2359304 | tf_op jit(solution)/shard_map/ppermute | solution.py:54
  38.7 21.5 %collective-permute-start.6 = (bf16[512,768]{1,0:T(8,128)(2,1)S(1)}, bf16[512,768]{1,0:T(8,128)(2,1)}, u32[]{:S(2)}, u32[]{:S(2)}) collective-permute-start(bf16[512,768]{1,0:T(8,128)(2,1)S(1)} %copy-done.1), channel_id=1, source_target_pairs={{0,1},{8,9},{16,17},{24,25},{32,33},{40,41},{48,49},{56,57},{64,65... | collective-permute-start | bytes 2359304 | tf_op jit(solution)/shard_map/ppermute | solution.py:54
  40.0 16.3 %collective-permute-start.7 = (bf16[384,768]{1,0:T(8,128)(2,1)}, bf16[384,768]{1,0:T(8,128)(2,1)}, u32[]{:S(2)}, u32[]{:S(2)}) collective-permute-start(bf16[384,768]{1,0:T(8,128)(2,1)} %copy-done.15), channel_id=1, source_target_pairs={{0,16},{8,56},{16,32},{24,8},{32,48},{40,24},{48,0},{56,40},{64,80... | collective-permute-start | bytes 1769480 | tf_op jit(solution)/shard_map/ppermute | solution.py:54
  42.6 16.9 %collective-permute-start.8 = (bf16[384,768]{1,0:T(8,128)(2,1)}, bf16[384,768]{1,0:T(8,128)(2,1)}, u32[]{:S(2)}, u32[]{:S(2)}) collective-permute-start(bf16[384,768]{1,0:T(8,128)(2,1)} %copy-done.15), channel_id=1, source_target_pairs={{0,48},{8,24},{16,0},{24,40},{32,16},{40,56},{48,32},{56,8},{64,11... | collective-permute-start | bytes 1769480 | tf_op jit(solution)/shard_map/ppermute | solution.py:54
  42.7 161.4 %all-gather.7.cloned.1.call-start = ((), (), s32[]{:S(2)}) async-start(), calls=%async_computation.1 | async-start | bytes 2654208 | tf_op jit(solution)/shard_map/all_gather | solution.py:429
  42.7 19.1 %copy-start.9 = (bf16[384,768]{1,0:T(8,128)(2,1)S(1)}, bf16[384,768]{1,0:T(8,128)(2,1)}, u32[]{:S(2)}) copy-start(bf16[384,768]{1,0:T(8,128)(2,1)} %copy-done.8) | copy-start | bytes 1769476
  60.1 1.5 copy-start.4
  61.7 14.6 %collective-permute-start.14 = (bf16[2,192,768]{2,1,0:T(8,128)(2,1)S(1)}, bf16[2,192,768]{2,1,0:T(8,128)(2,1)S(1)}, u32[]{:S(2)}, u32[]{:S(2)}) collective-permute-start(bf16[2,192,768]{2,1,0:T(8,128)(2,1)S(1)} %pad_maximum_fusion.1), channel_id=1, source_target_pairs={{0,48},{8,24},{16,0},{24,40},{32,16},{40,56},{48,32},{56,8},{64,11... | collective-permute-start | bytes 1769480 | tf_op jit(solution)/shard_map/ppermute | solution.py:54
  62.9 17.8 %collective-permute-start.13 = (bf16[2,192,768]{2,1,0:T(8,128)(2,1)S(1)}, bf16[2,192,768]{2,1,0:T(8,128)(2,1)S(1)}, u32[]{:S(2)}, u32[]{:S(2)}) collective-permute-start(bf16[2,192,768]{2,1,0:T(8,128)(2,1)S(1)} %pad_maximum_fusion), channel_id=1, source_target_pairs={{0,16},{8,56},{16,32},{24,8},{32,48},{40,24},{48,0},{56,40},{64,80... | collective-permute-start | bytes 1769480 | tf_op jit(solution)/shard_map/ppermute | solution.py:54
  76.3 4.3 %copy-start.2 = (bf16[2,192,768]{2,1,0:T(8,128)(2,1)}, bf16[2,192,768]{2,1,0:T(8,128)(2,1)S(1)}, u32[]{:S(2)}) copy-start(bf16[2,192,768]{2,1,0:T(8,128)(2,1)S(1)} %collective-permute-done.14.refs_3_.refs_5_) | copy-start | bytes 1769476
  80.6 0.8 copy-start.3
  84.5 24.1 %collective-permute-start.15 = (bf16[4,384,768]{2,1,0:T(8,128)(2,1)}, bf16[4,384,768]{2,1,0:T(8,128)(2,1)S(1)}, u32[]{:S(2)}, u32[]{:S(2)}) collective-permute-start(bf16[4,384,768]{2,1,0:T(8,128)(2,1)} %stack.27.refs_9_), channel_id=1, source_target_pairs={{0,8},{8,0},{16,24},{24,16},{32,40},{40,32},{48,56},{56,48},{64,72... | collective-permute-start | bytes 7077896 | tf_op jit(solution)/shard_map/ppermute | solution.py:54
  88.1 17.5 %collective-permute-start.10 = (bf16[512,768]{1,0:T(8,128)(2,1)}, bf16[512,768]{1,0:T(8,128)(2,1)S(1)}, u32[]{:S(2)}, u32[]{:S(2)}) collective-permute-start(bf16[512,768]{1,0:T(8,128)(2,1)} %collective-permute-done.6.refs_4_), channel_id=1, source_target_pairs={{0,2},{8,14},{16,18},{24,30},{32,34},{40,46},{48,50},{56,62},{64,6... | collective-permute-start | bytes 2359304 | tf_op jit(solution)/shard_map/ppermute | solution.py:54
  88.1 20.5 %collective-permute-start.11 = (bf16[512,768]{1,0:T(8,128)(2,1)}, bf16[512,768]{1,0:T(8,128)(2,1)S(1)}, u32[]{:S(2)}, u32[]{:S(2)}) collective-permute-start(bf16[512,768]{1,0:T(8,128)(2,1)} %collective-permute-done.6.refs_4_), channel_id=1, source_target_pairs={{0,6},{8,10},{16,22},{24,26},{32,38},{40,42},{48,54},{56,58},{64,7... | collective-permute-start | bytes 2359304 | tf_op jit(solution)/shard_map/ppermute | solution.py:54
  89.6 19.1 %collective-permute-start.12 = (bf16[512,768]{1,0:T(8,128)(2,1)}, bf16[512,768]{1,0:T(8,128)(2,1)S(1)}, u32[]{:S(2)}, u32[]{:S(2)}) collective-permute-start(bf16[512,768]{1,0:T(8,128)(2,1)} %collective-permute-done.5.refs_3_), channel_id=1, source_target_pairs={{0,1},{8,9},{16,17},{24,25},{32,33},{40,41},{48,49},{56,57},{64,65... | collective-permute-start | bytes 2359304 | tf_op jit(solution)/shard_map/ppermute | solution.py:54
  105.6 6.9 %copy-start.11 = (bf16[512,768]{1,0:T(8,128)(2,1)}, bf16[512,768]{1,0:T(8,128)(2,1)S(1)}, u32[]{:S(2)}) copy-start(bf16[512,768]{1,0:T(8,128)(2,1)S(1)} %collective-permute-done.10.refs_5_) | copy-start | bytes 2359300
  108.6 0.9 copy-start.12
  108.7 2.7 %copy-start.13 = (bf16[512,768]{1,0:T(8,128)(2,1)}, bf16[512,768]{1,0:T(8,128)(2,1)S(1)}, u32[]{:S(2)}) copy-start(bf16[512,768]{1,0:T(8,128)(2,1)S(1)} %collective-permute-done.12.refs_7_) | copy-start | bytes 2359300
  109.5 3.1 %copy-start.6 = (bf16[4,384,768]{2,1,0:T(8,128)(2,1)}, bf16[4,384,768]{2,1,0:T(8,128)(2,1)S(1)}, u32[]{:S(2)}) copy-start(bf16[4,384,768]{2,1,0:T(8,128)(2,1)S(1)} %collective-permute-done.15.refs_11_) | copy-start | bytes 7077892
  109.5 25.2 %collective-permute-start.16 = (bf16[384,384]{1,0:T(8,128)(2,1)}, bf16[384,384]{1,0:T(8,128)(2,1)S(1)}, u32[]{:S(2)}, u32[]{:S(2)}) collective-permute-start(bf16[384,384]{1,0:T(8,128)(2,1)} %param.23), channel_id=1, source_target_pairs={{0,0},{8,8},{16,1},{24,9},{32,2},{40,10},{48,3},{56,11},{64,4},{72... | collective-permute-start | bytes 884744 | tf_op jit(solution)/shard_map/ppermute | solution.py:54
  112.6 30.3 %copy-start.20 = (s32[16,27]{1,0:T(8,128)S(1)}, s32[16,27]{1,0:T(8,128)}, u32[]{:S(2)}) copy-start(s32[16,27]{1,0:T(8,128)} %param.27) | copy-start | bytes 5188
  112.6 31.3 %copy-start.21 = (pred[16,16]{1,0:T(8,128)(4,1)S(1)}, pred[16,16]{1,0:T(8,128)(4,1)}, u32[]{:S(2)}) copy-start(pred[16,16]{1,0:T(8,128)(4,1)} %constant.48.clone) | copy-start | bytes 772
  112.6 31.3 %copy-start.22 = (pred[16,16]{1,0:T(8,128)(4,1)S(1)}, pred[16,16]{1,0:T(8,128)(4,1)}, u32[]{:S(2)}) copy-start(pred[16,16]{1,0:T(8,128)(4,1)} %constant.49.clone) | copy-start | bytes 772
  134.7 0.7 copy-start.19
  135.5 10.5 %collective-permute-start.19 = (bf16[8,384,384]{2,1,0:T(8,128)(2,1)}, bf16[8,384,384]{2,1,0:T(8,128)(2,1)S(1)}, u32[]{:S(2)}, u32[]{:S(2)}) collective-permute-start(bf16[8,384,384]{2,1,0:T(8,128)(2,1)} %bitcast.28), channel_id=1, source_target_pairs={{0,8},{8,0},{16,24},{24,16},{32,40},{40,32},{48,56},{56,48},{64,72... | collective-permute-start | bytes 7077896 | tf_op jit(solution)/shard_map/ppermute | solution.py:54
  136.5 18.4 %collective-permute-start.17 = (bf16[512,768]{1,0:T(8,128)(2,1)}, bf16[512,768]{1,0:T(8,128)(2,1)S(1)}, u32[]{:S(2)}, u32[]{:S(2)}) collective-permute-start(bf16[512,768]{1,0:T(8,128)(2,1)} %get-tuple-element.78.refs_2_), channel_id=1, source_target_pairs={{0,8},{1,9},{2,10},{3,11},{4,12},{5,13},{6,14},{7,15},{8,16},{9,17... | collective-permute-start | bytes 2359304 | tf_op jit(solution)/shard_map/ppermute | solution.py:54
  140.9 14.3 %collective-permute-start.18 = (bf16[512,768]{1,0:T(8,128)(2,1)}, bf16[512,768]{1,0:T(8,128)(2,1)}, u32[]{:S(2)}, u32[]{:S(2)}) collective-permute-start(bf16[512,768]{1,0:T(8,128)(2,1)} %get-tuple-element.78.refs_2_), channel_id=1, source_target_pairs={{8,0},{9,1},{10,2},{11,3},{12,4},{13,5},{14,6},{15,7},{16,8},{17,9... | collective-permute-start | bytes 2359304 | tf_op jit(solution)/shard_map/ppermute | solution.py:54
  146.0 1.5 copy-start.5
  154.9 0.9 copy-start.14
  162.8 27.2 %collective-permute-start.20 = (bf16[512,384]{1,0:T(8,128)(2,1)}, bf16[512,384]{1,0:T(8,128)(2,1)S(1)}, u32[]{:S(2)}, u32[]{:S(2)}) collective-permute-start(bf16[512,384]{1,0:T(8,128)(2,1)} %attend.1.refs_0_), channel_id=1, source_target_pairs={{0,2},{8,14},{16,18},{24,30},{32,34},{40,46},{48,50},{56,62},{64,6... | collective-permute-start | bytes 1179656 | tf_op jit(solution)/shard_map/ppermute | solution.py:54
  175.1 15.0 %collective-permute-start.21 = (bf16[512,384]{1,0:T(8,128)(2,1)}, bf16[512,384]{1,0:T(8,128)(2,1)S(1)}, u32[]{:S(2)}, u32[]{:S(2)}) collective-permute-start(bf16[512,384]{1,0:T(8,128)(2,1)} %attend.1.refs_0_), channel_id=1, source_target_pairs={{0,6},{8,10},{16,22},{24,26},{32,38},{40,42},{48,54},{56,58},{64,7... | collective-permute-start | bytes 1179656 | tf_op jit(solution)/shard_map/ppermute | solution.py:54
  175.1 16.8 %collective-permute-start.22 = (bf16[512,384]{1,0:T(8,128)(2,1)}, bf16[512,384]{1,0:T(8,128)(2,1)S(1)}, u32[]{:S(2)}, u32[]{:S(2)}) collective-permute-start(bf16[512,384]{1,0:T(8,128)(2,1)} %attend.1.refs_0_), channel_id=1, source_target_pairs={{0,4},{8,12},{16,20},{24,28},{32,36},{40,44},{48,52},{56,60},{64,6... | collective-permute-start | bytes 1179656 | tf_op jit(solution)/shard_map/ppermute | solution.py:54
  176.3 17.5 %collective-permute-start.23 = (bf16[512,384]{1,0:T(8,128)(2,1)}, bf16[512,384]{1,0:T(8,128)(2,1)}, u32[]{:S(2)}, u32[]{:S(2)}) collective-permute-start(bf16[512,384]{1,0:T(8,128)(2,1)} %attend.1.refs_0_), channel_id=1, source_target_pairs={{0,1},{8,9},{16,17},{24,25},{32,33},{40,41},{48,49},{56,57},{64,65... | collective-permute-start | bytes 1179656 | tf_op jit(solution)/shard_map/ppermute | solution.py:54
  190.0 19.3 %copy-start.17 = (bf16[512,384]{1,0:T(8,128)(2,1)}, bf16[512,384]{1,0:T(8,128)(2,1)S(1)}, u32[]{:S(2)}) copy-start(bf16[512,384]{1,0:T(8,128)(2,1)S(1)} %collective-permute-done.20.refs_1_) | copy-start | bytes 1179652
  190.0 19.3 %copy-start.18 = (bf16[512,384]{1,0:T(8,128)(2,1)}, bf16[512,384]{1,0:T(8,128)(2,1)S(1)}, u32[]{:S(2)}) copy-start(bf16[512,384]{1,0:T(8,128)(2,1)S(1)} %collective-permute-done.21.refs_2_) | copy-start | bytes 1179652
  191.9 17.4 %copy-start.16 = (bf16[512,384]{1,0:T(8,128)(2,1)}, bf16[512,384]{1,0:T(8,128)(2,1)S(1)}, u32[]{:S(2)}) copy-start(bf16[512,384]{1,0:T(8,128)(2,1)S(1)} %collective-permute-done.22.refs_3_) | copy-start | bytes 1179652
  204.1 5.2 %collective-permute-start.27 = (bf16[8,384,384]{2,1,0:T(8,128)(2,1)}, bf16[8,384,384]{2,1,0:T(8,128)(2,1)S(1)}, u32[]{:S(2)}, u32[]{:S(2)}) collective-permute-start(bf16[8,384,384]{2,1,0:T(8,128)(2,1)} %bitcast.25), channel_id=1, source_target_pairs={{0,8},{8,0},{16,24},{24,16},{32,40},{40,32},{48,56},{56,48},{64,72... | collective-permute-start | bytes 7077896 | tf_op jit(solution)/shard_map/ppermute | solution.py:54
  204.9 11.8 %collective-permute-start.24 = (bf16[512,384]{1,0:T(8,128)(2,1)}, bf16[512,384]{1,0:T(8,128)(2,1)}, u32[]{:S(2)}, u32[]{:S(2)}) collective-permute-start(bf16[512,384]{1,0:T(8,128)(2,1)} %collective-permute-done.23.refs_4_), channel_id=1, source_target_pairs={{0,2},{8,14},{16,18},{24,30},{32,34},{40,46},{48,50},{56,62},{64,6... | collective-permute-start | bytes 1179656 | tf_op jit(solution)/shard_map/ppermute | solution.py:54
  207.3 10.5 %collective-permute-start.25 = (bf16[512,384]{1,0:T(8,128)(2,1)}, bf16[512,384]{1,0:T(8,128)(2,1)}, u32[]{:S(2)}, u32[]{:S(2)}) collective-permute-start(bf16[512,384]{1,0:T(8,128)(2,1)} %collective-permute-done.23.refs_4_), channel_id=1, source_target_pairs={{0,6},{8,10},{16,22},{24,26},{32,38},{40,42},{48,54},{56,58},{64,7... | collective-permute-start | bytes 1179656 | tf_op jit(solution)/shard_map/ppermute | solution.py:54
  207.3 10.5 %collective-permute-start.26 = (bf16[512,384]{1,0:T(8,128)(2,1)S(1)}, bf16[512,384]{1,0:T(8,128)(2,1)}, u32[]{:S(2)}, u32[]{:S(2)}) collective-permute-start(bf16[512,384]{1,0:T(8,128)(2,1)S(1)} %collective-permute-done.22.refs_3_), channel_id=1, source_target_pairs={{0,1},{8,9},{16,17},{24,25},{32,33},{40,41},{48,49},{56,57},{64,65... | collective-permute-start | bytes 1179656 | tf_op jit(solution)/shard_map/ppermute | solution.py:54
  209.3 1.4 copy-start
Sparse Core Ops, SparseCore 0:
  42.8 58.1 all-gather.4
  135.6 68.4 all-gather.6
